TPU v7x, 128 devices: a whole 4x4x4 slice. The times are simulated.
128 devices in a mesh: seq: 32 (over x, z_hi, y), head: 4 (over z_lo, core).
Axes of the slice: x: 4, y: 4, z: 4 (z_hi: 2, z_lo: 2; z = z_hi * 2 + z_lo), core: 2. Of those that a mesh axis runs over, the one named last changes fastest.
Arguments:
- residual_in: bfloat16 [4096, 4096], P(('seq', 'head')), may hold values from -3 to 3
- expert_hidden: bfloat16 [128, 128, 3, 1536], P(('seq', 'head')), may hold values from -6 to 6
- w_down: bfloat16 [128, 1536, 4096], P(('seq', 'head')), may hold values from -0.15625 to 0.15625
- routes: int32 [4096, 8], P(('seq', 'head')), may hold values from 0 to 127, all different within a row; in each aligned block of 32 rows (0 to 31, 32 to 63, ...) at most 3 rows name the same one
- gates: float32 [4096, 8], P(('seq', 'head')), may hold values from 0.05 to 0.3
- norm_gain: float32 [4096], replicated, may hold values from 0.1 to 1.9
- w_qkv: bfloat16 [4096, 4, 2304], P('seq', 'head'), may hold values from -0.09375 to 0.09375
- cache_kv: bfloat16 [12288, 4, 2, 128], P('seq', 'head'), may hold values from -600 to 600, as said below
Outputs:
- stream: bfloat16 [4096, 4096], P(('seq', 'head'))
- attended: bfloat16 [4096, 4, 2048], P('seq', 'head')
Inputs may be any that keep to these rules, and one draw needn't show every extreme that they name: `routes`: each token names 8 different experts. Among the 32 tokens of one owner no expert is named by more than 3 tokens, and in some owners one expert is named by exactly 3. `cache_kv`: cached keys already carry their rotary phase for positions 0 to 12287.
All inputs are finite; a program needn't handle non-finite values.
Results may differ from a plain program's by a relative error of at most 0.024.
The roundings to bfloat16 on the way count: a program that leaves them out, or rounds other values in their place, can miss the bound.
Values may be sent and summed in bfloat16 or wider, within the bound.
No kernel may reach another device: no remote copies, remote signals or barrier semaphores. Data moves between devices by JAX's collectives and lax.ppermute only.
A program may use at most 320 MiB of HBM per device.

v0:
```python
import jax
import jax.numpy as jnp
from jax import lax
from jax.sharding import PartitionSpec as P

rope_base = 1000000.0
masked_score = -1e30


def slot_numbers(route_block):
    flat_routes = route_block.reshape(-1)
    per_token = route_block.shape[1]
    token_of = jnp.arange(flat_routes.shape[0], dtype=jnp.int32) // per_token
    earlier = (flat_routes[:, None] == flat_routes[None, :]) & (
        token_of[None, :] < token_of[:, None]
    )
    return jnp.sum(earlier.astype(jnp.int32), axis=1).reshape(route_block.shape)


def rotate(values, positions):
    half_dim = values.shape[-1] // 2
    inverse = rope_base ** (-2.0 * jnp.arange(half_dim, dtype=jnp.float32) / values.shape[-1])
    angles = positions[:, None] * inverse[None, :]
    cosine = jnp.cos(angles)[:, None, :]
    sine_part = jnp.sin(angles)[:, None, :]
    first_half = values[..., :half_dim]
    second_half = values[..., half_dim:]
    return jnp.concatenate(
        [
            first_half * cosine - second_half * sine_part,
            second_half * cosine + first_half * sine_part,
        ],
        axis=-1,
    )


def attend(carried, query_rows, block_kv, allowed, inv_root):
    running_max, running_sum, running_out = carried
    scores = (
        jnp.einsum("qd,rd->qr", query_rows, block_kv[:, 0], preferred_element_type=jnp.float32)
        * inv_root
    )
    if allowed is not None:
        scores = jnp.where(allowed, scores, masked_score)
    new_max = jnp.maximum(running_max, jnp.max(scores, axis=1))
    weights = jnp.exp(scores - new_max[:, None])
    if allowed is not None:
        weights = jnp.where(allowed, weights, 0.0)
    factor = jnp.exp(running_max - new_max)
    new_sum = running_sum * factor + jnp.sum(weights, axis=1)
    new_out = running_out * factor[:, None] + jnp.dot(
        weights.astype(jnp.bfloat16), block_kv[:, 1], preferred_element_type=jnp.float32
    )
    return (new_max, new_sum, new_out)


def body(residual_in, expert_hidden, w_down, routes, gates, norm_gain, w_qkv, cache_kv):
    slot_cap = expert_hidden.shape[2]
    model_width = w_down.shape[2]
    head_dim = cache_kv.shape[3]
    produced = jnp.einsum(
        "ocf,fd->ocd", expert_hidden[0], w_down[0], preferred_element_type=jnp.float32
    ).astype(jnp.bfloat16)
    returned = lax.all_to_all(produced, ("seq", "head"), split_axis=0, concat_axis=0, tiled=True)
    token_count, per_token = routes.shape
    row_index = (routes * slot_cap + slot_numbers(routes)).reshape(-1)
    picked = jnp.take(returned.reshape(-1, model_width), row_index, axis=0).reshape(
        token_count, per_token, model_width
    )
    moe_out = jnp.sum(gates[:, :, None] * picked.astype(jnp.float32), axis=1)
    stream = (residual_in.astype(jnp.float32) + moe_out).astype(jnp.bfloat16)
    widened = lax.optimization_barrier(stream).astype(jnp.float32)
    inverse_rms = lax.rsqrt(jnp.mean(widened * widened, axis=1, keepdims=True) + 1e-06)
    normed = (widened * inverse_rms * norm_gain[None, :]).astype(jnp.bfloat16)
    group_rows = lax.all_gather(normed, "head", axis=0, tiled=True)
    tok_seq = group_rows.shape[0]
    qkv_width = w_qkv.shape[2]
    projected = jnp.dot(
        group_rows,
        lax.all_gather(w_qkv, "seq", axis=0, tiled=True)[:, 0, :],
        preferred_element_type=jnp.float32,
    )
    per_kv = qkv_width // head_dim - 2
    span_first = lax.axis_index("seq") * tok_seq
    span_index = span_first + jnp.arange(tok_seq, dtype=jnp.int32)
    cache_length = cache_kv.shape[0] * lax.axis_size("seq")
    positions = (span_index + cache_length).astype(jnp.float32)
    heads_out = projected.reshape(tok_seq, per_kv + 2, head_dim)
    queries = (
        rotate(heads_out[:, :per_kv], positions)
        .astype(jnp.bfloat16)
        .reshape(tok_seq * per_kv, head_dim)
    )
    new_keys = rotate(heads_out[:, per_kv : per_kv + 1], positions)
    span_kv = jnp.concatenate([new_keys, heads_out[:, per_kv + 1 :]], axis=1).astype(jnp.bfloat16)
    query_index = jnp.repeat(span_index, per_kv)
    inv_root = head_dim ** (-0.5)
    row_total = tok_seq * per_kv
    carried = (
        jnp.full((row_total,), masked_score, jnp.float32),
        jnp.zeros((row_total,), jnp.float32),
        jnp.zeros((row_total, head_dim), jnp.float32),
    )
    carried = attend(
        carried, queries, lax.all_gather(cache_kv, "seq", axis=0, tiled=True)[:, 0], None, inv_root
    )
    key_rows = lax.all_gather(span_kv, "seq", axis=0, tiled=True)
    key_index = jnp.arange(key_rows.shape[0], dtype=jnp.int32)
    allowed = key_index[None, :] <= query_index[:, None]
    carried = attend(carried, queries, key_rows, allowed, inv_root)
    attended = (
        (carried[2] / carried[1][:, None])
        .astype(jnp.bfloat16)
        .reshape(tok_seq, 1, per_kv * head_dim)
    )
    return (stream, attended)


def solution(mesh):
    in_specs = (
        P(("seq", "head"), None),
        P(("seq", "head"), None, None, None),
        P(("seq", "head"), None, None),
        P(("seq", "head"), None),
        P(("seq", "head"), None),
        P(),
        P("seq", "head", None),
        P("seq", "head", None, None),
    )
    out_specs = (P(("seq", "head"), None), P("seq", "head", None))
    return jax.shard_map(body, mesh=mesh, in_specs=in_specs, out_specs=out_specs, check_vma=False)
```

profile of v0, /device:TPU:6, one launch (start us, length us, event | category | flops | bytes accessed | tf_op | source)
XLA Modules:
  0.0 536.5 jit_solution(14758680274253219516)
XLA Ops:
  7.2 0.7 all-gather.7.cloned.1.call-update
  7.9 0.5 copy-done
  8.4 9.8 %fusion.11 = bf16[128,3,4096]{2,0,1:T(8,128)(2,1)S(1)} fusion(bf16[1,1536,4096]{2,1,0:T(8,128)(2,1)} %param.10, bf16[1,128,3,1536]{3,1,2,0:T(8,128)(2,1)S(1)} %copy-done), kind=kOutput, calls=%fused_computation.15 | convolution fusion | flops 4833411072 | bytes 16908288 | tf_op jit(solution)/shard_map/ocf,fd->ocd/dot_general | solution.py:61
  18.3 4.7 copy.32
  23.0 10.9 %all-to-all-start = ((bf16[128,3,4096]{2,1,0:T(4,128)(2,1)}), bf16[128,3,4096]{2,1,0:T(4,128)(2,1)}, u32[]{:S(2)}, u32[]{:S(2)}) async-start(bf16[128,3,4096]{2,1,0:T(4,128)(2,1)} %copy.32), calls=%async_computation | async-start | bytes 8388608 | tf_op jit(solution)/shard_map/all_to_all | solution.py:64
  34.7 57.4 %all-to-all-done = bf16[128,3,4096]{2,1,0:T(4,128)(2,1)} async-done(((bf16[128,3,4096]{2,1,0:T(4,128)(2,1)}), bf16[128,3,4096]{2,1,0:T(4,128)(2,1)}, u32[]{:S(2)}, u32[]{:S(2)}) %all-to-all-start) | async-done | bytes 3145760 | tf_op jit(solution)/shard_map/all_to_all | solution.py:64
  92.1 6.0 %reshape.237 = bf16[384,4096]{1,0:T(8,128)(2,1)S(1)} reshape(bf16[128,3,4096]{2,1,0:T(4,128)(2,1)} %all-to-all-done) | data formatting | bytes 6291456 | tf_op jit(solution)/shard_map/reshape | solution.py:67
  98.1 3.1 gather_fusion
  101.2 3.5 multiply_reduce_fusion.1
  105.6 0.8 fusion.36
  106.5 1.7 copy.36
  108.8 111.0 %all-gather.7.cloned.1.call-done = bf16[4096,1,2304]{2,0,1:T(8,128)(2,1)} async-done(((bf16[128,1,2304]{2,0,1:T(8,128)(2,1)}), bf16[4096,1,2304]{2,0,1:T(8,128)(2,1)}) %all-gather.7.cloned.1.call-update) | async-done | bytes 18874384 | tf_op jit(solution)/shard_map/all_gather | solution.py:80
  219.8 23.1 %copy.33 = bf16[2304,4096]{1,0:T(8,128)(2,1)} copy(bf16[2304,4096]{0,1:T(8,128)(2,1)} %bitcast.46) | data formatting | bytes 37748736 | tf_op jit(solution)/shard_map/dot_general | solution.py:78
  242.9 9.3 %fusion.32 = f32[128,18,128]{0,2,1:T(8,128)S(1)} fusion(bf16[18,128,4096]{2,1,0:T(8,128)(2,1)} %bitcast.45, bf16[128,4096]{1,0:T(8,128)(2,1)} %all-gather.5.cloned.1.call-done), kind=kOutput, calls=%fused_computation.30 | convolution fusion | flops 2415919104 | bytes 21102592 | tf_op jit(solution)/shard_map/dot_general | solution.py:78
  253.5 0.6 pad_maximum_fusion.3
  254.2 82.9 %all-gather.9.cloned.1.call-done = bf16[12288,1,2,128]{3,0,2,1:T(8,128)(2,1)} async-done(((bf16[384,1,2,128]{3,0,2,1:T(8,128)(2,1)}), bf16[12288,1,2,128]{3,0,2,1:T(8,128)(2,1)}) %all-gather.9.cloned.1.call-update) | async-done | bytes 6291472 | tf_op jit(solution)/shard_map/all_gather | solution.py:105
  337.1 36.6 %multiply_reduce_fusion = (f32[2048]{0:T(1024)S(1)}, f32[2048,12288]{1,0:T(8,128)}) fusion(bf16[12288,2,128]{2,0,1:T(8,128)(2,1)} %bitcast.51, bf16[2048,64]{1,0:T(8,128)(2,1)S(1)} %bitcast.49, bf16[2048,64]{1,0:T(8,128)(2,1)S(1)} %bitcast.47), kind=kOutput, calls=%fused_computation.2 | convolution fusion | flops 6493829120 | bytes 104341504 | tf_op jit(solution)/shard_map/qd,rd->qr/dot_general | solution.py:40
  373.7 41.3 %all-gather.11.cloned.1.call-done = bf16[4096,2,128]{0,2,1:T(8,128)(2,1)} async-done(((bf16[128,2,128]{0,2,1:T(8,128)(2,1)}), bf16[4096,2,128]{0,2,1:T(8,128)(2,1)}) %all-gather.11.cloned.1.call-update) | async-done | bytes 2097168 | tf_op jit(solution)/shard_map/all_gather | solution.py:107
  415.0 15.2 %fusion.4 = (f32[2048]{0:T(1024)S(1)}, f32[2048,4096]{1,0:T(8,128)}) fusion(s32[2048]{0:T(1024)S(1)} %le.30, bf16[4096,2,128]{0,2,1:T(8,128)(2,1)} %all-gather.11.cloned.1.call-done, bf16[2048,64]{1,0:T(8,128)(2,1)S(1)} %bitcast.50, bf16[2048,64]{1,0:T(8,128)(2,1)S(1)} %bitcast.48), kind=kOutput, calls=%fused_computation.9 | convolution fusion | flops 2182084608 | bytes 35143680 | tf_op jit(solution)/shard_map/qd,rd->qr/dot_general | solution.py:40
  430.3 16.3 %fusion.5 = f32[2048]{0:T(1024)S(1)} fusion(f32[2048,4096]{1,0:T(8,128)} %get-tuple-element.18, f32[2048]{0:T(1024)S(1)} %get-tuple-element.11, s32[2048]{0:T(1024)S(1)} %le.30), kind=kLoop, calls=%fused_computation.10 | loop fusion | flops 50329600 | bytes 33579008 | tf_op jit(solution)/shard_map/reduce_sum | solution.py:50
  446.6 31.1 %fusion = f32[2048]{0:T(1024)S(1)} fusion(f32[2048,12288]{1,0:T(8,128)} %get-tuple-element.16, f32[2048]{0:T(1024)S(1)} %get-tuple-element.12), kind=kLoop, calls=%fused_computation.3 | loop fusion | flops 75495424 | bytes 100679680 | tf_op jit(solution)/shard_map/reduce_sum | solution.py:50
  477.7 35.5 %fusion.21 = f32[2048,128]{1,0:T(8,128)} fusion(bf16[12288,2,128]{2,0,1:T(8,128)(2,1)} %bitcast.52, f32[2048,12288]{1,0:T(8,128)} %get-tuple-element.16, f32[2048]{0:T(1024)S(1)} %get-tuple-element.12, f32[2048]{0:T(1024)S(1)} %get-tuple-element.3, f32[2048]{0:T(1024)S(1)} %get-tuple-element.10), kind=kOutput, calls=%fused_computation.22 | convolution fusion | flops 6518472704 | bytes 104882176 | tf_op jit(solution)/shard_map/dot_general | solution.py:51
  513.3 15.7 %fusion.27 = bf16[2048,128]{1,0:T(8,128)(2,1)S(1)} fusion(f32[2048,128]{1,0:T(8,128)} %fusion.21, f32[2048,4096]{1,0:T(8,128)} %get-tuple-element.18, f32[2048]{0:T(1024)S(1)} %get-tuple-element.11, s32[2048]{0:T(1024)S(1)} %le.30, bf16[4096,2,128]{0,2,1:T(8,128)(2,1)} %all-gather.11.cloned.1.call-done, f32[2048]{0:T(1024)S(1)} %get-tuple-element.2), kind=kOutput, calls=%fused_computation.25 | convolution fusion | flops 2198601728 | bytes 36200448 | tf_op jit(solution)/shard_map/dot_general | solution.py:51
  529.0 1.0 reshape.239
  (47 shorter events, 3.5 us)
Async XLA Ops:
  7.2 1.3 copy-start
  7.2 212.7 %all-gather.7.cloned.1.call-start = ((), (), s32[]{:S(2)}) async-start(), calls=%async_computation.2 | async-start | bytes 19464192 | tf_op jit(solution)/shard_map/all_gather | solution.py:80
  8.4 25.6 %copy-start.5 = (s32[32,8]{0,1:T(8,128)S(1)}, s32[32,8]{0,1:T(8,128)}, u32[]{:S(2)}) copy-start(s32[32,8]{0,1:T(8,128)} %param.11) | copy-start | bytes 3076
  8.4 26.2 %copy-start.6 = (f32[32,8]{0,1:T(8,128)S(1)}, f32[32,8]{0,1:T(8,128)}, u32[]{:S(2)}) copy-start(f32[32,8]{0,1:T(8,128)} %param.12) | copy-start | bytes 3076
  23.0 81.7 %copy-start.3 = (bf16[32,4096]{1,0:T(8,128)(2,1)S(1)}, bf16[32,4096]{1,0:T(8,128)(2,1)}, u32[]{:S(2)}) copy-start(bf16[32,4096]{1,0:T(8,128)(2,1)} %param.8) | copy-start | bytes 786436
  23.0 82.5 %copy-start.4 = (f32[4096]{0:T(1024)S(1)}, f32[4096]{0:T(1024)}, u32[]{:S(2)}) copy-start(f32[4096]{0:T(1024)} %param.13) | copy-start | bytes 49156
  23.0 69.1 %all-to-all-start = ((bf16[128,3,4096]{2,1,0:T(4,128)(2,1)}), bf16[128,3,4096]{2,1,0:T(4,128)(2,1)}, u32[]{:S(2)}, u32[]{:S(2)}) async-start(bf16[128,3,4096]{2,1,0:T(4,128)(2,1)} %copy.32), calls=%async_computation | async-start | bytes 8388608 | tf_op jit(solution)/shard_map/all_to_all | solution.py:64
  34.0 209.0 %all-gather.5.cloned.1.call-start = ((), (), s32[]{:S(2)}) async-start(), calls=%async_computation.1 | async-start | bytes 1310720 | tf_op jit(solution)/shard_map/all_gather | solution.py:75
  104.9 0.7 copy-start.2
  106.4 230.7 %all-gather.9.cloned.1.call-start = ((), (), s32[]{:S(2)}) async-start(), calls=%async_computation.3 | async-start | bytes 6488064 | tf_op jit(solution)/shard_map/all_gather | solution.py:105
  108.2 306.8 %all-gather.11.cloned.1.call-start = ((), (), s32[]{:S(2)}) async-start(), calls=%async_computation.4 | async-start | bytes 2162688 | tf_op jit(solution)/shard_map/all_gather | solution.py:107
  513.3 16.8 %copy-start.1 = (bf16[1,128,3,1536]{3,1,2,0:T(8,128)(2,1)S(1)}, bf16[1,128,3,1536]{3,1,2,0:T(8,128)(2,1)}, u32[]{:S(2)}) copy-start(bf16[1,128,3,1536]{3,1,2,0:T(8,128)(2,1)} %param.9) | copy-start | bytes 3538948
Sparse Core Ops, SparseCore 0:
  11.1 208.7 all-gather.6
  222.1 18.3 all-gather.4
  243.5 93.5 all-gather.8
  340.3 74.7 all-gather.10
where the time goes:
time: 538 us; the launch traced here: 537 us
  waiting for transfers between devices  293 us (54%)
  matrix products  122 us (23%)
  other arithmetic  53.5 us (10%)
  local copies, waits for them, and re-layouts  42.2 us (8%)
  between operations  14 us (3%)
  starting transfers between devices  11.3 us (2%)
    all_gather x1, waiting for transfers between devices, body(): lax.all_gather(w_qkv, 'seq', axis=0, tiled=True)[:, 0, :]  111 us
    all_gather x1, waiting for transfers between devices, body(): lax.all_gather(cache_kv, 'seq', axis=0, tiled=True)[:, 0]  82.9 us
    all_to_all x1, waiting for transfers between devices, body(): lax.all_to_all(produced, ('seq', 'head'), split_axis=0, concat_axis=0, ti...  57.4 us
    dot_general x2, matrix products, attend(): jnp.einsum('qd,rd->qr', query_rows, block_kv[:, 0], preferred_element_typ...  51.9 us
    dot_general x2, matrix products, attend(): jnp.dot(weights.astype(jnp.bfloat16), block_kv[:, 1], preferred_element_t...  51.2 us
    reduce_sum x2, other arithmetic, attend(): new_sum = running_sum * factor + jnp.sum(weights, axis=1)  47.4 us
    all_gather x1, waiting for transfers between devices, body(): key_rows = lax.all_gather(span_kv, 'seq', axis=0, tiled=True)  41.3 us
    dot_general x1, local copies, waits for them, and re-layouts, body(): jnp.dot(group_rows, lax.all_gather(w_qkv, 'seq', axis=0, tiled=True)[:, 0...  23.1 us
  transfers between devices with their start and end apart: 5, of which 4 were waited for; matrix products, arithmetic and copies ran while one was open for 19% of the time, Pallas kernels for 0%

commit v1 on v0

v1 whole, which is shorter than its diff:
```python
import functools

import jax
import jax.numpy as jnp
from jax import lax
from jax.experimental import pallas as pl
from jax.experimental.pallas import tpu as pltpu
from jax.sharding import Mesh, PartitionSpec as P

rope_base = 1000000.0
masked_score = -1e30
log2_e = 1.4426950408889634

token_axes = ("x", "zh", "y", "zl", "c")
seq_axes = ("x", "zh", "y")
head_axes = ("zl", "c")

MIB = 2**20
column_parts = 8


def slot_numbers(route_block):
    flat_routes = route_block.reshape(-1)
    per_token = route_block.shape[1]
    token_of = jnp.arange(flat_routes.shape[0], dtype=jnp.int32) // per_token
    earlier = (flat_routes[:, None] == flat_routes[None, :]) & (
        token_of[None, :] < token_of[:, None]
    )
    return jnp.sum(earlier.astype(jnp.int32), axis=1).reshape(route_block.shape)


def expert_kernel(x_ref, w_ref, o_ref, scratch):
    step = pl.program_id(0)
    rows = x_ref.shape[0]
    product = jnp.dot(x_ref[...], w_ref[...], preferred_element_type=jnp.float32)
    for lane in range(product.shape[1] // 128):
        scratch[lane, pl.ds(step, rows, stride=column_parts), :] = product[
            :, lane * 128 : (lane + 1) * 128
        ]

    @pl.when(step == column_parts - 1)
    def _():
        for lane in range(product.shape[1] // 128):
            o_ref[:, lane * 128 : (lane + 1) * 128] = scratch[lane].astype(jnp.bfloat16)


def expert_rows(hidden, weight):
    rows, depth = hidden.shape
    width = weight.shape[1]
    part = width // column_parts
    return pl.pallas_call(
        expert_kernel,
        grid=(column_parts,),
        in_specs=[
            pl.BlockSpec((rows, depth), lambda b: (0, 0)),
            pl.BlockSpec((depth, part), lambda b: (0, b)),
        ],
        out_specs=pl.BlockSpec((rows * column_parts, part), lambda b: (0, 0)),
        out_shape=jax.ShapeDtypeStruct((rows * column_parts, part), jnp.bfloat16),
        scratch_shapes=[pltpu.VMEM((part // 128, rows * column_parts, 128), jnp.float32)],
        compiler_params=pltpu.CompilerParams(vmem_limit_bytes=40 * MIB),
        cost_estimate=pl.CostEstimate(
            flops=2 * rows * depth * width,
            bytes_accessed=2 * (depth * width + rows * (depth + width)),
            transcendentals=0,
        ),
    )(hidden, weight)


def combine_kernel(row_ref, gate_ref, got_ref, res_ref, gain_ref, stream_ref, normed_ref, scratch):
    tokens, width = res_ref.shape
    per_token = row_ref.shape[0] // tokens
    part = got_ref.shape[2]

    def one(t, carry):
        total = jnp.zeros((column_parts, part), jnp.float32)
        for k in range(per_token):
            at = t * per_token + k
            total = total + gate_ref[at] * got_ref[row_ref[at]].astype(jnp.float32)
        first = pl.multiple_of(t * column_parts, column_parts)
        for lane in range(part // 128):
            scratch[lane, pl.ds(first, column_parts), :] = total[:, lane * 128 : (lane + 1) * 128]
        return carry

    lax.fori_loop(0, tokens, one, 0)
    squares = jnp.zeros((tokens, 128), jnp.float32)
    for b in range(column_parts):
        for lane in range(part // 128):
            cols = pl.ds(b * part + lane * 128, 128)
            moe = scratch[lane, pl.ds(b, tokens, stride=column_parts), :]
            stream = (res_ref[:, cols].astype(jnp.float32) + moe).astype(jnp.bfloat16)
            stream_ref[:, cols] = stream
            widened = stream.astype(jnp.float32)
            squares = squares + widened * widened
    mean = jnp.sum(squares, axis=1, keepdims=True) * (1.0 / width)
    inverse_rms = lax.rsqrt(mean + 1e-06)
    for b in range(width // 512):
        cols = pl.ds(b * 512, 512)
        widened = stream_ref[:, cols].astype(jnp.float32)
        normed_ref[:, cols] = (widened * inverse_rms * gain_ref[:, cols]).astype(jnp.bfloat16)


def combine(row_index, gates, returned, residual, gain):
    tokens, width = residual.shape
    part = returned.shape[2]
    vmem = pl.BlockSpec(memory_space=pltpu.VMEM)
    smem = pl.BlockSpec(memory_space=pltpu.SMEM)
    return pl.pallas_call(
        combine_kernel,
        in_specs=[smem, smem, vmem, vmem, vmem],
        out_specs=[vmem, vmem],
        out_shape=[jax.ShapeDtypeStruct((tokens, width), jnp.bfloat16)] * 2,
        scratch_shapes=[pltpu.VMEM((part // 128, tokens * column_parts, 128), jnp.float32)],
        compiler_params=pltpu.CompilerParams(vmem_limit_bytes=32 * MIB),
        cost_estimate=pl.CostEstimate(
            flops=20 * tokens * width, bytes_accessed=4 * MIB, transcendentals=0
        ),
    )(row_index, gates, returned, residual, gain)


def project_kernel(blocks, pieces, place_ref, shard_ref, *refs):
    normed_refs = refs[:blocks]
    piece_refs = refs[blocks : blocks + pieces]
    cos_ref, sin_ref, kept_ref, sent_ref, rows_scr, weight_scr, total, sems = refs[blocks + pieces :]
    copies = [
        pltpu.make_async_copy(piece_refs[p], weight_scr.at[p], sems.at[p]) for p in range(pieces)
    ]
    for copy in copies:
        copy.start()
    height = normed_refs[0].shape[0]
    for b in range(blocks):
        first = pl.multiple_of(place_ref[b], 32)
        rows_scr[pl.ds(first, height), :] = normed_refs[b][...]
    per_piece = piece_refs[0].shape[0] // 128
    for p in range(pieces):
        copies[p].wait()
        left = jnp.concatenate(
            [
                rows_scr[:, pl.ds(pl.multiple_of(shard_ref[p * per_piece + u] * 128, 128), 128)]
                for u in range(per_piece)
            ],
            axis=1,
        )
        part = jnp.dot(left, weight_scr[p], preferred_element_type=jnp.float32)
        if p == 0:
            total[...] = part
        else:
            total[...] += part
    heads = total.shape[1] // 128
    tokens = kept_ref.shape[0]
    for half, out_ref in ((0, kept_ref), (1, sent_ref)):
        rows = pl.ds(half * tokens, tokens)
        for h in range(heads):
            table = 1 if h == heads - 1 else 0
            cosine = cos_ref[table, rows, :]
            sine = sin_ref[table, rows, :]
            head = total[rows, h * 128 : (h + 1) * 128]
            turned = pltpu.roll(head, 64, 1)
            out_ref[:, h * 128 : (h + 1) * 128] = (head * cosine + turned * sine).astype(
                jnp.bfloat16
            )


def project(places, shards, normed_blocks, pieces, cosine, sine):
    blocks, count = len(normed_blocks), len(pieces)
    height, width = normed_blocks[0].shape
    depth, columns = pieces[0].shape
    rows = blocks * height
    vmem = pl.BlockSpec(memory_space=pltpu.VMEM)
    smem = pl.BlockSpec(memory_space=pltpu.SMEM)
    hbm = pl.BlockSpec(memory_space=pl.ANY)
    return pl.pallas_call(
        functools.partial(project_kernel, blocks, count),
        in_specs=[smem, smem] + [vmem] * blocks + [hbm] * count + [vmem] * 2,
        out_specs=[vmem, vmem],
        out_shape=[jax.ShapeDtypeStruct((rows // 2, columns), jnp.bfloat16)] * 2,
        scratch_shapes=[
            pltpu.VMEM((rows, width), jnp.bfloat16),
            pltpu.VMEM((count, depth, columns), jnp.bfloat16),
            pltpu.VMEM((rows, columns), jnp.float32),
            pltpu.SemaphoreType.DMA((count,)),
        ],
        compiler_params=pltpu.CompilerParams(vmem_limit_bytes=40 * MIB),
        cost_estimate=pl.CostEstimate(
            flops=2 * rows * width * columns, bytes_accessed=2 * width * columns, transcendentals=0
        ),
    )(places, shards, *normed_blocks, *pieces, cosine, sine)


query_chunk = 512
key_chunk = 1024


def split_queries(q_ref, turned, scale):
    for j in range(q_ref.shape[1] // 128):
        cols = pl.ds(j * 128, 128)
        scaled = q_ref[:, cols].astype(jnp.float32).T * scale
        high = scaled.astype(jnp.bfloat16)
        turned[:128, cols] = high
        turned[128:, cols] = (scaled - high.astype(jnp.float32)).astype(jnp.bfloat16)


def attend_block(turned, kv_ref, m_ref, l_ref, acc_ref, allowed):
    keys = kv_ref[:, :128]
    doubled = jnp.concatenate([keys, keys], axis=1)
    jobs = [
        (c, k)
        for k in range(kv_ref.shape[0] // key_chunk)
        for c in range(turned.shape[1] // query_chunk)
    ]

    def score(job):
        c, k = job
        return jnp.dot(
            doubled[k * key_chunk : (k + 1) * key_chunk],
            turned[:, pl.ds(c * query_chunk, query_chunk)],
            preferred_element_type=jnp.float32,
        )

    following = score(jobs[0])
    for n, (c, k) in enumerate(jobs):
        s = following
        if n + 1 < len(jobs):
            following = score(jobs[n + 1])
        cols = pl.ds(c * query_chunk, query_chunk)
        if allowed is not None:
            s = jnp.where(allowed(c, k), s, masked_score)
        m_old = m_ref[:, cols]
        m_new = jnp.maximum(m_old, jnp.max(s, axis=0, keepdims=True))
        factor = jnp.exp2(m_old - m_new)
        weights = jnp.exp2(s - m_new)
        m_ref[:, cols] = m_new
        l_ref[:, cols] = l_ref[:, cols] * factor + jnp.sum(weights, axis=0, keepdims=True)
        out = lax.dot_general(
            kv_ref[pl.ds(k * key_chunk, key_chunk), 128:],
            weights.astype(jnp.bfloat16),
            (((0,), (0,)), ((), ())),
            preferred_element_type=jnp.float32,
        )
        acc_ref[:, cols] = acc_ref[:, cols] * factor + out


def cache_kernel(scale, q_ref, kv_ref, m_ref, l_ref, acc_ref, turned):
    @pl.when(pl.program_id(0) == 0)
    def _():
        split_queries(q_ref, turned, scale)
        m_ref[...] = jnp.full_like(m_ref, masked_score)
        l_ref[...] = jnp.zeros_like(l_ref)
        acc_ref[...] = jnp.zeros_like(acc_ref)

    attend_block(turned, kv_ref, m_ref, l_ref, acc_ref, None)


def attend_cache(queries, cached, scale, block):
    tokens, width = queries.shape
    steps = cached.shape[0] // block
    whole = lambda i: (0, 0)
    return pl.pallas_call(
        functools.partial(cache_kernel, scale),
        grid=(steps,),
        in_specs=[
            pl.BlockSpec((tokens, width), whole),
            pl.BlockSpec((block, 256), lambda i: (i, 0)),
        ],
        out_specs=[
            pl.BlockSpec((1, tokens * width // 128), whole),
            pl.BlockSpec((1, tokens * width // 128), whole),
            pl.BlockSpec((128, tokens * width // 128), whole),
        ],
        out_shape=[
            jax.ShapeDtypeStruct((1, tokens * width // 128), jnp.float32),
            jax.ShapeDtypeStruct((1, tokens * width // 128), jnp.float32),
            jax.ShapeDtypeStruct((128, tokens * width // 128), jnp.float32),
        ],
        scratch_shapes=[pltpu.VMEM((256, tokens * width // 128), jnp.bfloat16)],
        compiler_params=pltpu.CompilerParams(vmem_limit_bytes=52 * MIB),
        cost_estimate=pl.CostEstimate(
            flops=8 * tokens * width * cached.shape[0],
            bytes_accessed=512 * cached.shape[0],
            transcendentals=tokens * width // 128 * cached.shape[0],
        ),
    )(queries, cached)


def span_kernel(
    scale, block, span_ref, q_ref, kv_ref, m_in, l_in, acc_in, o_ref, turned, m_ref, l_ref, acc_ref
):
    step = pl.program_id(0)
    tokens = q_ref.shape[0]
    first_query = span_ref[0] * tokens
    first_key = step * block

    @pl.when(step == 0)
    def _():
        split_queries(q_ref, turned, scale)
        m_ref[...] = m_in[...]
        l_ref[...] = l_in[...]
        acc_ref[...] = acc_in[...]

    @pl.when(first_key + block <= first_query)
    def _():
        attend_block(turned, kv_ref, m_ref, l_ref, acc_ref, None)

    def allowed(c, k):
        shape = (key_chunk, query_chunk)
        key = lax.broadcasted_iota(jnp.int32, shape, 0) + (first_key + k * key_chunk - first_query)
        token = lax.broadcasted_iota(jnp.int32, shape, 1) % tokens
        return key <= token

    @pl.when((first_key + block > first_query) & (first_key < first_query + tokens))
    def _():
        attend_block(turned, kv_ref, m_ref, l_ref, acc_ref, allowed)

    @pl.when(step == pl.num_programs(0) - 1)
    def _():
        for j in range(q_ref.shape[1] // 128):
            cols = pl.ds(j * 128, 128)
            o_ref[:, cols] = (acc_ref[:, cols] / l_ref[:, cols]).T.astype(jnp.bfloat16)


def attend_span(span, queries, keys_values, state, scale, block):
    tokens, width = queries.shape
    rows = tokens * width // 128
    steps = keys_values.shape[0] // block
    whole = lambda i, span_ref: (0, 0)
    needed = lambda i, span_ref: (
        jnp.minimum(i, (span_ref[0] * tokens + tokens - 1) // block),
        0,
    )
    return pl.pallas_call(
        functools.partial(span_kernel, scale, block),
        grid_spec=pltpu.PrefetchScalarGridSpec(
            num_scalar_prefetch=1,
            grid=(steps,),
            in_specs=[
                pl.BlockSpec((tokens, width), whole),
                pl.BlockSpec((block, 256), needed),
                pl.BlockSpec((1, rows), whole),
                pl.BlockSpec((1, rows), whole),
                pl.BlockSpec((128, rows), whole),
            ],
            out_specs=pl.BlockSpec((tokens, width), whole),
            scratch_shapes=[
                pltpu.VMEM((256, rows), jnp.bfloat16),
                pltpu.VMEM((1, rows), jnp.float32),
                pltpu.VMEM((1, rows), jnp.float32),
                pltpu.VMEM((128, rows), jnp.float32),
            ],
        ),
        out_shape=jax.ShapeDtypeStruct((tokens, width), jnp.bfloat16),
        compiler_params=pltpu.CompilerParams(vmem_limit_bytes=52 * MIB),
        cost_estimate=pl.CostEstimate(
            flops=8 * tokens * width * keys_values.shape[0],
            bytes_accessed=512 * keys_values.shape[0],
            transcendentals=rows * keys_values.shape[0],
        ),
    )(span, queries, keys_values, *state)


def shift(block, axis, by, size=4):
    return lax.ppermute(block, axis, [(i, (i + by) % size) for i in range(size)])


def ring_small(block, axis):
    return [shift(block, axis, 1), shift(block, axis, -1), shift(block, axis, 2)]


def ring_large(top, bottom, axis):
    before = [shift(top, axis, 1), shift(bottom, axis, 1)]
    after = [shift(top, axis, -1), shift(bottom, axis, -1)]
    opposite = [shift(before[0], axis, 1), shift(after[1], axis, -1)]
    return [top, bottom] + before + after + opposite


ring_steps = (0, -1, 1, 2)


def gather_weight(block, first_axis, second_axis):
    ring = [block] + ring_small(block, first_axis)
    top = jnp.concatenate(ring[:2], axis=0)
    bottom = jnp.concatenate(ring[2:], axis=0)
    return ring_large(top, bottom, second_axis)


def shard_order(first_is_x, x, zh, y):
    order = []
    for outer in ring_steps:
        for inner in ring_steps:
            dx, dy = (inner, outer) if first_is_x else (outer, inner)
            order.append(((x + dx) % 4) * 8 + zh * 4 + (y + dy) % 4)
    return order


def body(residual_in, expert_hidden, w_down, routes, gates, norm_gain, w_qkv, cache_kv):
    x, zh, y = lax.axis_index("x"), lax.axis_index("zh"), lax.axis_index("y")
    zl, core = lax.axis_index("zl"), lax.axis_index("c")
    seq_index = lax.axis_index(seq_axes)
    slot_cap = expert_hidden.shape[2]
    head_dim = cache_kv.shape[3]
    token_count, per_token = routes.shape
    seq_size = lax.axis_size(seq_axes)
    cache_length = cache_kv.shape[0] * seq_size
    tok_seq = token_count * lax.axis_size(head_axes)

    half_columns = w_qkv.shape[2] // 2
    weight_rows = w_qkv[:, 0, :]
    own_half = lax.dynamic_slice_in_dim(weight_rows, zh * half_columns, half_columns, axis=1)
    other_half = lax.dynamic_slice_in_dim(weight_rows, (1 - zh) * half_columns, half_columns, axis=1)
    partner_half = shift(other_half, "zh", 1, 2)
    pieces = gather_weight(own_half, "x", "y") + gather_weight(partner_half, "y", "x")
    shards = jnp.stack(shard_order(True, x, zh, y) + shard_order(False, x, 1 - zh, y))

    cached = lax.all_gather(cache_kv.reshape(-1, 2 * head_dim), seq_axes, axis=0, tiled=True)

    hidden = expert_hidden[0].reshape(-1, expert_hidden.shape[3])
    produced = expert_rows(hidden, w_down[0])
    returned = lax.all_to_all(produced, token_axes, split_axis=0, concat_axis=0, tiled=True)

    row_index = (routes * slot_cap + slot_numbers(routes)).reshape(-1)
    stream, normed = combine(
        row_index,
        gates.reshape(-1),
        returned.reshape(-1, column_parts, returned.shape[1]),
        residual_in,
        norm_gain[None, :],
    )

    z = zh * 2 + zl
    near = [normed] + [shift(normed, ("zh", "zl"), by) for by in (1, -1, 2)]
    far = [shift(block, "c", 1, 2) for block in near]
    places = []
    for c in (core, 1 - core):
        for by in ring_steps:
            source = (z + by) % 4
            other_span = ((source // 2) != zh).astype(jnp.int32)
            places.append(other_span * tok_seq + (source % 2) * 64 + c * 32)
    places = jnp.stack(places)

    half_dim = head_dim // 2
    inverse = rope_base ** (-2.0 * jnp.arange(half_dim, dtype=jnp.float32) / head_dim)
    partner_index = x * 8 + (1 - zh) * 4 + y
    steps = jnp.arange(tok_seq, dtype=jnp.int32)
    span_index = jnp.concatenate([seq_index * tok_seq + steps, partner_index * tok_seq + steps])
    angles = (span_index + cache_length).astype(jnp.float32)[:, None] * inverse[None, :]
    cosine = jnp.cos(angles)
    sine = jnp.sin(angles)
    cosine = jnp.concatenate([cosine, cosine], axis=1)
    sine = jnp.concatenate([-sine, sine], axis=1)
    plain = zh == 1
    cosine = jnp.stack([cosine, jnp.where(plain, 1.0, cosine)])
    sine = jnp.stack([sine, jnp.where(plain, 0.0, sine)])

    kept, sent = project(places, shards, near + far, pieces, cosine, sine)
    received = shift(sent, "zh", 1, 2)
    lower = jnp.where(zh == 0, kept, received)
    upper = jnp.where(zh == 0, received, kept)
    span_kv = upper[:, half_columns - 2 * head_dim :]
    queries = jnp.concatenate([lower, upper[:, : half_columns - 2 * head_dim]], axis=1)
    key_rows = lax.all_gather(span_kv, seq_axes, axis=0, tiled=True)

    scale = head_dim ** (-0.5) * log2_e
    state = attend_cache(queries, cached, scale, 2048)
    attended = attend_span(seq_index[None], queries, key_rows, state, scale, 1024)
    return (stream, attended[:, None, :])


def solution(mesh):
    fine = Mesh(mesh.devices.reshape(4, 2, 4, 2, 2), token_axes)
    in_specs = (
        P(token_axes, None),
        P(token_axes, None, None, None),
        P(token_axes, None, None),
        P(token_axes, None),
        P(token_axes, None),
        P(),
        P(seq_axes, head_axes, None),
        P(seq_axes, head_axes, None, None),
    )
    out_specs = (P(token_axes, None), P(seq_axes, head_axes, None))
    return jax.shard_map(body, mesh=fine, in_specs=in_specs, out_specs=out_specs, check_vma=False)
```

time: 538 us -> 301 us (0.56)
  waiting for transfers between devices: 293 us -> 154 us
  matrix products: 122 us -> 0 us
  Pallas kernels: 0 us -> 67.7 us
  other arithmetic: 53.5 us -> 6.03 us
  starting transfers between devices: 11.3 us -> 44.5 us
  local copies, waits for them, and re-layouts: 42.2 us -> 13.5 us
    all_gather x4 -> x2, waiting for transfers between devices: 235 us -> 35.3 us  [the longest x1 35.3 us: body(): key_rows = lax.all_gather(span_kv, seq_axes, axis=0, tiled=True)]
    dot_general x6 -> x0, matrix products: 122 us -> none  [the longest x2 51.9 us: attend(): jnp.einsum('qd,rd->qr', query_rows, block_kv[:, 0], preferred_element_typ...]
    ppermute x0 -> x27, waiting for transfers between devices: none -> 119 us  [shift(): lax.ppermute(block, axis, [(i, (i + by) % size) for i in range(size)])]
    pallas_call x0 -> x5, Pallas kernels: none -> 67.7 us  [the longest x1 32.3 us: attend_cache(): pl.pallas_call(functools.partial(cache_kernel, scale), grid=(steps,), in_...]
    all_to_all x1, waiting for transfers between devices: 57.4 us -> 0.01 us  [body(): lax.all_to_all(produced, token_axes, split_axis=0, concat_axis=0, tiled=T...]
    reduce_sum x4 -> x0, other arithmetic: 51.1 us -> none  [the longest x2 47.4 us: attend(): new_sum = running_sum * factor + jnp.sum(weights, axis=1)]
    ppermute x0 -> x27, starting transfers between devices: none -> 33.9 us  [shift(): lax.ppermute(block, axis, [(i, (i + by) % size) for i in range(size)])]
    dot_general x1 -> x0, local copies, waits for them, and re-layouts: 23.1 us -> none  [body(): jnp.dot(group_rows, lax.all_gather(w_qkv, 'seq', axis=0, tiled=True)[:, 0...]
  transfers between devices with their start and end apart: 5 -> 30, of which waited for: 4 -> 14; matrix products, arithmetic and copies ran while one was open for 19% -> 5% of each run, Pallas kernels for 0% -> 18%
where the time goes in v1:
time: 301 us; the launch traced here: 300 us
  waiting for transfers between devices  154 us (51%)
  Pallas kernels  67.7 us (22%)
  starting transfers between devices  44.5 us (15%)
  between operations  14.6 us (5%)
  local copies, waits for them, and re-layouts  13.5 us (4%)
  other arithmetic  6.03 us (2%)
    ppermute x27, waiting for transfers between devices, shift(): lax.ppermute(block, axis, [(i, (i + by) % size) for i in range(size)])  119 us
    all_gather x1, waiting for transfers between devices, body(): key_rows = lax.all_gather(span_kv, seq_axes, axis=0, tiled=True)  35.3 us
    ppermute x27, starting transfers between devices, shift(): lax.ppermute(block, axis, [(i, (i + by) % size) for i in range(size)])  33.9 us
    pallas_call x1, Pallas kernels, attend_cache(): pl.pallas_call(functools.partial(cache_kernel, scale), grid=(steps,), in_...  32.3 us
    pallas_call x1, Pallas kernels, attend_span(): pl.pallas_call(functools.partial(span_kernel, scale, block), grid_spec=pl...  14.1 us
    pallas_call x1, Pallas kernels, expert_rows(): pl.pallas_call(expert_kernel, grid=(column_parts,), in_specs=[pl.BlockSpe...  10.9 us
    all_to_all x1, starting transfers between devices, body(): lax.all_to_all(produced, token_axes, split_axis=0, concat_axis=0, tiled=T...  10.5 us
    pallas_call x1, Pallas kernels, project(): pl.pallas_call(functools.partial(project_kernel, blocks, count), in_specs...  8.15 us
  transfers between devices with their start and end apart: 30, of which 14 were waited for; matrix products, arithmetic and copies ran while one was open for 5% of the time, Pallas kernels for 18%

profile of v1, /device:TPU:6, one launch (start us, length us, event | category | flops | bytes accessed | tf_op | source)
XLA Modules:
  0.0 300.3 jit_solution(4068396797499817129)
XLA Ops:
  12.2 10.9 %shard_map.95 = bf16[3072,512]{1,0:T(8,128)(2,1)S(1)} custom-call(bf16[384,1536]{1,0:T(8,128)(2,1)S(1)} %reshape_squeeze.3.x_ref, bf16[1536,4096]{1,0:T(8,128)(2,1)} %bitcast.70), custom_call_target="tpu_custom_call" | custom-call | flops 4831838208 | bytes 16908288 | tf_op jit(solution)/shard_map/pallas_call | solution.py:51
  24.8 10.5 %all-to-all-start = ((bf16[128,24,512]{2,1,0:T(8,128)(2,1)}), bf16[128,24,512]{2,1,0:T(8,128)(2,1)S(1)}, u32[]{:S(2)}, u32[]{:S(2)}) async-start(bf16[128,24,512]{2,1,0:T(8,128)(2,1)} %bitcast.66), calls=%async_computation | async-start | bytes 6291456 | tf_op jit(solution)/shard_map/all_to_all | solution.py:417
  37.5 2.9 collective-permute-start.16
  43.3 35.3 %collective-permute-done.7 = bf16[128,1152]{1,0:T(8,128)(2,1)S(1)} collective-permute-done((bf16[128,1152]{1,0:T(8,128)(2,1)S(1)}, bf16[128,1152]{1,0:T(8,128)(2,1)S(1)}, u32[]{:S(2)}, u32[]{:S(2)}) %collective-permute-start.7) | collective-permute-done | bytes 294944 | tf_op jit(solution)/shard_map/ppermute | solution.py:361
  82.8 3.9 %collective-permute-done.16 = bf16[128,1152]{1,0:T(8,128)(2,1)S(1)} collective-permute-done((bf16[128,1152]{1,0:T(8,128)(2,1)S(1)}, bf16[128,1152]{1,0:T(8,128)(2,1)S(1)}, u32[]{:S(2)}, u32[]{:S(2)}) %collective-permute-start.16) | collective-permute-done | bytes 294944 | tf_op jit(solution)/shard_map/ppermute | solution.py:361
  86.7 3.2 %collective-permute-start.18 = (bf16[128,1152]{1,0:T(8,128)(2,1)S(1)}, bf16[128,1152]{1,0:T(8,128)(2,1)S(1)}, u32[]{:S(2)}, u32[]{:S(2)}) collective-permute-start(bf16[128,1152]{1,0:T(8,128)(2,1)S(1)} %collective-permute-done.16), channel_id=1, source_target_pairs={{0,12},{4,0},{8,4},{12,8},{1,13},{5,1},{9,5},{13,9},{2,14},{6,2},{... | collective-permute-start | bytes 884744 | tf_op jit(solution)/shard_map/ppermute | solution.py:361
  92.1 17.7 %collective-permute-done.18 = bf16[128,1152]{1,0:T(8,128)(2,1)S(1)} collective-permute-done((bf16[128,1152]{1,0:T(8,128)(2,1)S(1)}, bf16[128,1152]{1,0:T(8,128)(2,1)S(1)}, u32[]{:S(2)}, u32[]{:S(2)}) %collective-permute-start.18) | collective-permute-done | bytes 294944 | tf_op jit(solution)/shard_map/ppermute | solution.py:361
  111.5 17.9 %collective-permute-done.17 = bf16[128,1152]{1,0:T(8,128)(2,1)S(1)} collective-permute-done((bf16[128,1152]{1,0:T(8,128)(2,1)S(1)}, bf16[128,1152]{1,0:T(8,128)(2,1)S(1)}, u32[]{:S(2)}, u32[]{:S(2)}) %collective-permute-start.17) | collective-permute-done | bytes 294944 | tf_op jit(solution)/shard_map/ppermute | solution.py:361
  131.1 7.7 %collective-permute-done.19 = bf16[128,1152]{1,0:T(8,128)(2,1)S(1)} collective-permute-done((bf16[128,1152]{1,0:T(8,128)(2,1)S(1)}, bf16[128,1152]{1,0:T(8,128)(2,1)S(1)}, u32[]{:S(2)}, u32[]{:S(2)}) %collective-permute-start.19) | collective-permute-done | bytes 294944 | tf_op jit(solution)/shard_map/ppermute | solution.py:361
  138.8 3.4 %collective-permute-start.20 = (bf16[256,1152]{1,0:T(8,128)(2,1)}, bf16[256,1152]{1,0:T(8,128)(2,1)}, u32[]{:S(2)}, u32[]{:S(2)}) collective-permute-start(bf16[256,1152]{1,0:T(8,128)(2,1)} %constant_dynamic-update-slice_fusion.2.refs_16_), channel_id=1, source_target_pairs={{0,32},{32,64},{64,96},{96,0},{1,33},{33,65},{65,97},{97,1},{2,34}... | collective-permute-start | bytes 1769480 | tf_op jit(solution)/shard_map/ppermute | solution.py:361
  145.6 3.4 %collective-permute-done.13.refs_13_ = bf16[256,1152]{1,0:T(8,128)(2,1)} collective-permute-done((bf16[256,1152]{1,0:T(8,128)(2,1)}, bf16[256,1152]{1,0:T(8,128)(2,1)}, u32[]{:S(2)}, u32[]{:S(2)}) %collective-permute-start.13) | collective-permute-done | bytes 589856 | tf_op jit(solution)/shard_map/ppermute | solution.py:361
  149.1 7.3 %collective-permute-done.20.refs_18_ = bf16[256,1152]{1,0:T(8,128)(2,1)} collective-permute-done((bf16[256,1152]{1,0:T(8,128)(2,1)}, bf16[256,1152]{1,0:T(8,128)(2,1)}, u32[]{:S(2)}, u32[]{:S(2)}) %collective-permute-start.20) | collective-permute-done | bytes 589856 | tf_op jit(solution)/shard_map/ppermute | solution.py:361
  156.3 8.3 %collective-permute-done.21.refs_19_ = bf16[256,1152]{1,0:T(8,128)(2,1)} collective-permute-done((bf16[256,1152]{1,0:T(8,128)(2,1)}, bf16[256,1152]{1,0:T(8,128)(2,1)}, u32[]{:S(2)}, u32[]{:S(2)}) %collective-permute-start.21) | collective-permute-done | bytes 589856 | tf_op jit(solution)/shard_map/ppermute | solution.py:361
  164.7 3.7 %collective-permute-start.24 = (bf16[256,1152]{1,0:T(8,128)(2,1)}, bf16[256,1152]{1,0:T(8,128)(2,1)}, u32[]{:S(2)}, u32[]{:S(2)}) collective-permute-start(bf16[256,1152]{1,0:T(8,128)(2,1)} %collective-permute-done.20.refs_18_), channel_id=1, source_target_pairs={{0,32},{32,64},{64,96},{96,0},{1,33},{33,65},{65,97},{97,1},{2,34}... | collective-permute-start | bytes 1769480 | tf_op jit(solution)/shard_map/ppermute | solution.py:361
  170.1 2.3 shard_map.96
  172.4 3.8 %collective-permute-start = (bf16[32,4096]{1,0:T(8,128)(2,1)}, bf16[32,4096]{1,0:T(8,128)(2,1)S(1)}, u32[]{:S(2)}, u32[]{:S(2)}) collective-permute-start(bf16[32,4096]{1,0:T(8,128)(2,1)} %get-tuple-element.10.refs_0_), channel_id=1, source_target_pairs={{0,2},{2,16},{16,18},{18,0},{1,3},{3,17},{17,19},{19,1},{4,6},{6,2... | collective-permute-start | bytes 786440 | tf_op jit(solution)/shard_map/ppermute | solution.py:361
  177.9 2.9 collective-permute-start.2
  185.7 2.9 collective-permute-done.2.refs_3_
  190.2 4.1 %collective-permute-done.25.refs_23_ = bf16[256,1152]{1,0:T(8,128)(2,1)S(1)} collective-permute-done((bf16[256,1152]{1,0:T(8,128)(2,1)}, bf16[256,1152]{1,0:T(8,128)(2,1)S(1)}, u32[]{:S(2)}, u32[]{:S(2)}) %collective-permute-start.25) | collective-permute-done | bytes 589856 | tf_op jit(solution)/shard_map/ppermute | solution.py:361
  194.3 8.1 %shard_map.97 = (bf16[128,1152]{1,0:T(8,128)(2,1)S(1)}, bf16[128,1152]{1,0:T(8,128)(2,1)S(1)}) custom-call(s32[8]{0:T(128)S(1)} %stack.148.place_ref, s32[32]{0:T(128)S(1)} %stack.181.shard_ref, bf16[32,4096]{1,0:T(8,128)(2,1)} %get-tuple-element.10.refs_0_, bf16[32,4096]{1,0:T(8,128)(2,1)S(1)} %collective-permute-done.refs_1_, ...), custom_call_target="tpu_custom_call" | custom-call | flops 2415919104 | bytes 9437184 | tf_op jit(solution)/shard_map/pallas_call | solution.py:172
  203.1 7.9 %collective-permute-done.26 = bf16[128,1152]{1,0:T(8,128)(2,1)S(1)} collective-permute-done((bf16[128,1152]{1,0:T(8,128)(2,1)S(1)}, bf16[128,1152]{1,0:T(8,128)(2,1)S(1)}, u32[]{:S(2)}, u32[]{:S(2)}) %collective-permute-start.26) | collective-permute-done | bytes 294944 | tf_op jit(solution)/shard_map/ppermute | solution.py:361
  211.8 32.3 %shard_map.98 = (f32[1,2048]{1,0:T(1,128)S(1)}, f32[1,2048]{1,0:T(1,128)S(1)}, f32[128,2048]{1,0:T(8,128)S(1)}) custom-call(bf16[128,2048]{1,0:T(8,128)(2,1)S(1)} %pad_maximum_fusion.1.q_ref, bf16[12288,256]{1,0:T(8,128)(2,1)} %all-gather.5.cloned.1.call-done.kv_ref), custom_call_target="tpu_custom_call" | custom-call | flops 25769803776 | bytes 6291456 | tf_op jit(solution)/shard_map/pallas_call | solution.py:258
  244.1 35.3 %all-gather.3.cloned.1.call-done.kv_ref = bf16[4096,256]{1,0:T(8,128)(2,1)} async-done(((bf16[128,256]{1,0:T(8,128)(2,1)}), bf16[4096,256]{1,0:T(8,128)(2,1)}) %all-gather.3.cloned.1.call-update) | async-done | bytes 2097168 | tf_op jit(solution)/shard_map/all_gather | solution.py:459
  279.4 14.1 %shard_map.99 = bf16[128,2048]{1,0:T(8,128)(2,1)} custom-call(s32[1]{0:T(128)} %bitcast.4.span_ref, bf16[128,2048]{1,0:T(8,128)(2,1)S(1)} %pad_maximum_fusion.1.q_ref, bf16[4096,256]{1,0:T(8,128)(2,1)} %all-gather.3.cloned.1.call-done.kv_ref, f32[1,2048]{1,0:T(1,128)S(1)} %get-tuple-element.13.m_in, f32[1,2048]{1,0:T(1,128)S(1)} %get-tuple-element.14.l_in, ...), custom_call_target="tpu_custom_call" | custom-call | flops 8589934592 | bytes 2097152 | tf_op jit(solution)/shard_map/pallas_call | solution.py:330
  (91 shorter events, 36.0 us)
Async XLA Ops:
  7.2 204.7 %all-gather.5.cloned.1.call-start = ((), (), s32[]{:S(2)}) async-start(), calls=%async_computation.2 | async-start | bytes 6488064 | tf_op jit(solution)/shard_map/all_gather | solution.py:413
  24.8 145.3 %all-to-all-start = ((bf16[128,24,512]{2,1,0:T(8,128)(2,1)}), bf16[128,24,512]{2,1,0:T(8,128)(2,1)S(1)}, u32[]{:S(2)}, u32[]{:S(2)}) async-start(bf16[128,24,512]{2,1,0:T(8,128)(2,1)} %bitcast.66), calls=%async_computation | async-start | bytes 6291456 | tf_op jit(solution)/shard_map/all_to_all | solution.py:417
  35.2 244.1 %all-gather.3.cloned.1.call-start = ((), (), s32[]{:S(2)}) async-start(), calls=%async_computation.1 | async-start | bytes 2162688 | tf_op jit(solution)/shard_map/all_gather | solution.py:459
  36.4 42.3 %collective-permute-start.7 = (bf16[128,1152]{1,0:T(8,128)(2,1)S(1)}, bf16[128,1152]{1,0:T(8,128)(2,1)S(1)}, u32[]{:S(2)}, u32[]{:S(2)}) collective-permute-start(bf16[128,1152]{1,0:T(8,128)(2,1)S(1)} %get-tuple-element.19), channel_id=1, source_target_pairs={{0,32},{32,64},{64,96},{96,0},{1,33},{33,65},{65,97},{97,1},{2,34}... | collective-permute-start | bytes 884744 | tf_op jit(solution)/shard_map/ppermute | solution.py:361
  37.5 49.1 %collective-permute-start.16 = (bf16[128,1152]{1,0:T(8,128)(2,1)S(1)}, bf16[128,1152]{1,0:T(8,128)(2,1)S(1)}, u32[]{:S(2)}, u32[]{:S(2)}) collective-permute-start(bf16[128,1152]{1,0:T(8,128)(2,1)S(1)} %get-tuple-element.18), channel_id=1, source_target_pairs={{0,16},{16,0},{1,17},{17,1},{2,18},{18,2},{3,19},{19,3},{4,20},{20... | collective-permute-start | bytes 884744 | tf_op jit(solution)/shard_map/ppermute | solution.py:361
  40.4 49.5 %collective-permute-start.8 = (bf16[128,1152]{1,0:T(8,128)(2,1)S(1)}, bf16[128,1152]{1,0:T(8,128)(2,1)S(1)}, u32[]{:S(2)}, u32[]{:S(2)}) collective-permute-start(bf16[128,1152]{1,0:T(8,128)(2,1)S(1)} %get-tuple-element.19), channel_id=1, source_target_pairs={{0,96},{32,0},{64,32},{96,64},{1,97},{33,1},{65,33},{97,65},{2,98}... | collective-permute-start | bytes 884744 | tf_op jit(solution)/shard_map/ppermute | solution.py:361
  41.9 48.7 %collective-permute-start.9 = (bf16[128,1152]{1,0:T(8,128)(2,1)S(1)}, bf16[128,1152]{1,0:T(8,128)(2,1)S(1)}, u32[]{:S(2)}, u32[]{:S(2)}) collective-permute-start(bf16[128,1152]{1,0:T(8,128)(2,1)S(1)} %get-tuple-element.19), channel_id=1, source_target_pairs={{0,64},{32,96},{64,0},{96,32},{1,65},{33,97},{65,1},{97,33},{2,66}... | collective-permute-start | bytes 884744 | tf_op jit(solution)/shard_map/ppermute | solution.py:361
  79.6 63.4 %collective-permute-start.10 = (bf16[256,1152]{1,0:T(8,128)(2,1)}, bf16[256,1152]{1,0:T(8,128)(2,1)}, u32[]{:S(2)}, u32[]{:S(2)}) collective-permute-start(bf16[256,1152]{1,0:T(8,128)(2,1)} %pad_maximum_fusion.refs_8_), channel_id=1, source_target_pairs={{0,4},{4,8},{8,12},{12,0},{1,5},{5,9},{9,13},{13,1},{2,6},{6,10},{... | collective-permute-start | bytes 1769480 | tf_op jit(solution)/shard_map/ppermute | solution.py:361
  81.0 64.5 %collective-permute-start.12 = (bf16[256,1152]{1,0:T(8,128)(2,1)}, bf16[256,1152]{1,0:T(8,128)(2,1)}, u32[]{:S(2)}, u32[]{:S(2)}) collective-permute-start(bf16[256,1152]{1,0:T(8,128)(2,1)} %pad_maximum_fusion.refs_8_), channel_id=1, source_target_pairs={{0,12},{4,0},{8,4},{12,8},{1,13},{5,1},{9,5},{13,9},{2,14},{6,2},{... | collective-permute-start | bytes 1769480 | tf_op jit(solution)/shard_map/ppermute | solution.py:361
  86.7 23.1 %collective-permute-start.18 = (bf16[128,1152]{1,0:T(8,128)(2,1)S(1)}, bf16[128,1152]{1,0:T(8,128)(2,1)S(1)}, u32[]{:S(2)}, u32[]{:S(2)}) collective-permute-start(bf16[128,1152]{1,0:T(8,128)(2,1)S(1)} %collective-permute-done.16), channel_id=1, source_target_pairs={{0,12},{4,0},{8,4},{12,8},{1,13},{5,1},{9,5},{13,9},{2,14},{6,2},{... | collective-permute-start | bytes 884744 | tf_op jit(solution)/shard_map/ppermute | solution.py:361
  91.3 52.2 %collective-permute-start.11 = (bf16[256,1152]{1,0:T(8,128)(2,1)}, bf16[256,1152]{1,0:T(8,128)(2,1)}, u32[]{:S(2)}, u32[]{:S(2)}) collective-permute-start(bf16[256,1152]{1,0:T(8,128)(2,1)} %constant_dynamic-update-slice_fusion.refs_9_), channel_id=1, source_target_pairs={{0,4},{4,8},{8,12},{12,0},{1,5},{5,9},{9,13},{13,1},{2,6},{6,10},{... | collective-permute-start | bytes 1769480 | tf_op jit(solution)/shard_map/ppermute | solution.py:361
  91.3 38.1 %collective-permute-start.17 = (bf16[128,1152]{1,0:T(8,128)(2,1)S(1)}, bf16[128,1152]{1,0:T(8,128)(2,1)S(1)}, u32[]{:S(2)}, u32[]{:S(2)}) collective-permute-start(bf16[128,1152]{1,0:T(8,128)(2,1)S(1)} %collective-permute-done.16), channel_id=1, source_target_pairs={{0,4},{4,8},{8,12},{12,0},{1,5},{5,9},{9,13},{13,1},{2,6},{6,10},{... | collective-permute-start | bytes 884744 | tf_op jit(solution)/shard_map/ppermute | solution.py:361
  109.8 29.0 %collective-permute-start.19 = (bf16[128,1152]{1,0:T(8,128)(2,1)S(1)}, bf16[128,1152]{1,0:T(8,128)(2,1)S(1)}, u32[]{:S(2)}, u32[]{:S(2)}) collective-permute-start(bf16[128,1152]{1,0:T(8,128)(2,1)S(1)} %collective-permute-done.16), channel_id=1, source_target_pairs={{0,8},{4,12},{8,0},{12,4},{1,9},{5,13},{9,1},{13,5},{2,10},{6,14},... | collective-permute-start | bytes 884744 | tf_op jit(solution)/shard_map/ppermute | solution.py:361
  129.4 19.6 %collective-permute-start.13 = (bf16[256,1152]{1,0:T(8,128)(2,1)}, bf16[256,1152]{1,0:T(8,128)(2,1)}, u32[]{:S(2)}, u32[]{:S(2)}) collective-permute-start(bf16[256,1152]{1,0:T(8,128)(2,1)} %constant_dynamic-update-slice_fusion.refs_9_), channel_id=1, source_target_pairs={{0,12},{4,0},{8,4},{12,8},{1,13},{5,1},{9,5},{13,9},{2,14},{6,2},{... | collective-permute-start | bytes 1769480 | tf_op jit(solution)/shard_map/ppermute | solution.py:361
  138.8 17.5 %collective-permute-start.20 = (bf16[256,1152]{1,0:T(8,128)(2,1)}, bf16[256,1152]{1,0:T(8,128)(2,1)}, u32[]{:S(2)}, u32[]{:S(2)}) collective-permute-start(bf16[256,1152]{1,0:T(8,128)(2,1)} %constant_dynamic-update-slice_fusion.2.refs_16_), channel_id=1, source_target_pairs={{0,32},{32,64},{64,96},{96,0},{1,33},{33,65},{65,97},{97,1},{2,34}... | collective-permute-start | bytes 1769480 | tf_op jit(solution)/shard_map/ppermute | solution.py:361
  143.0 21.7 %collective-permute-start.21 = (bf16[256,1152]{1,0:T(8,128)(2,1)}, bf16[256,1152]{1,0:T(8,128)(2,1)}, u32[]{:S(2)}, u32[]{:S(2)}) collective-permute-start(bf16[256,1152]{1,0:T(8,128)(2,1)} %constant_dynamic-update-slice_fusion.4.refs_17_), channel_id=1, source_target_pairs={{0,32},{32,64},{64,96},{96,0},{1,33},{33,65},{65,97},{97,1},{2,34}... | collective-permute-start | bytes 1769480 | tf_op jit(solution)/shard_map/ppermute | solution.py:361
  143.5 29.0 %collective-permute-start.22 = (bf16[256,1152]{1,0:T(8,128)(2,1)}, bf16[256,1152]{1,0:T(8,128)(2,1)}, u32[]{:S(2)}, u32[]{:S(2)}) collective-permute-start(bf16[256,1152]{1,0:T(8,128)(2,1)} %constant_dynamic-update-slice_fusion.2.refs_16_), channel_id=1, source_target_pairs={{0,96},{32,0},{64,32},{96,64},{1,97},{33,1},{65,33},{97,65},{2,98}... | collective-permute-start | bytes 1769480 | tf_op jit(solution)/shard_map/ppermute | solution.py:361
  145.6 30.7 %collective-permute-start.23 = (bf16[256,1152]{1,0:T(8,128)(2,1)}, bf16[256,1152]{1,0:T(8,128)(2,1)}, u32[]{:S(2)}, u32[]{:S(2)}) collective-permute-start(bf16[256,1152]{1,0:T(8,128)(2,1)} %constant_dynamic-update-slice_fusion.4.refs_17_), channel_id=1, source_target_pairs={{0,96},{32,0},{64,32},{96,64},{1,97},{33,1},{65,33},{97,65},{2,98}... | collective-permute-start | bytes 1769480 | tf_op jit(solution)/shard_map/ppermute | solution.py:361
  149.0 28.9 %collective-permute-start.14 = (bf16[256,1152]{1,0:T(8,128)(2,1)}, bf16[256,1152]{1,0:T(8,128)(2,1)}, u32[]{:S(2)}, u32[]{:S(2)}) collective-permute-start(bf16[256,1152]{1,0:T(8,128)(2,1)} %collective-permute-done.10.refs_10_), channel_id=1, source_target_pairs={{0,4},{4,8},{8,12},{12,0},{1,5},{5,9},{9,13},{13,1},{2,6},{6,10},{... | collective-permute-start | bytes 1769480 | tf_op jit(solution)/shard_map/ppermute | solution.py:361
  156.3 24.6 %collective-permute-start.15 = (bf16[256,1152]{1,0:T(8,128)(2,1)}, bf16[256,1152]{1,0:T(8,128)(2,1)}, u32[]{:S(2)}, u32[]{:S(2)}) collective-permute-start(bf16[256,1152]{1,0:T(8,128)(2,1)} %collective-permute-done.13.refs_13_), channel_id=1, source_target_pairs={{0,12},{4,0},{8,4},{12,8},{1,13},{5,1},{9,5},{13,9},{2,14},{6,2},{... | collective-permute-start | bytes 1769480 | tf_op jit(solution)/shard_map/ppermute | solution.py:361
  164.7 18.5 %collective-permute-start.24 = (bf16[256,1152]{1,0:T(8,128)(2,1)}, bf16[256,1152]{1,0:T(8,128)(2,1)}, u32[]{:S(2)}, u32[]{:S(2)}) collective-permute-start(bf16[256,1152]{1,0:T(8,128)(2,1)} %collective-permute-done.20.refs_18_), channel_id=1, source_target_pairs={{0,32},{32,64},{64,96},{96,0},{1,33},{33,65},{65,97},{97,1},{2,34}... | collective-permute-start | bytes 1769480 | tf_op jit(solution)/shard_map/ppermute | solution.py:361
  172.4 12.8 %collective-permute-start = (bf16[32,4096]{1,0:T(8,128)(2,1)}, bf16[32,4096]{1,0:T(8,128)(2,1)S(1)}, u32[]{:S(2)}, u32[]{:S(2)}) collective-permute-start(bf16[32,4096]{1,0:T(8,128)(2,1)} %get-tuple-element.10.refs_0_), channel_id=1, source_target_pairs={{0,2},{2,16},{16,18},{18,0},{1,3},{3,17},{17,19},{19,1},{4,6},{6,2... | collective-permute-start | bytes 786440 | tf_op jit(solution)/shard_map/ppermute | solution.py:361
  180.9 13.4 %collective-permute-start.25 = (bf16[256,1152]{1,0:T(8,128)(2,1)}, bf16[256,1152]{1,0:T(8,128)(2,1)S(1)}, u32[]{:S(2)}, u32[]{:S(2)}) collective-permute-start(bf16[256,1152]{1,0:T(8,128)(2,1)} %collective-permute-done.23.refs_21_), channel_id=1, source_target_pairs={{0,96},{32,0},{64,32},{96,64},{1,97},{33,1},{65,33},{97,65},{2,98}... | collective-permute-start | bytes 1769480 | tf_op jit(solution)/shard_map/ppermute | solution.py:361
  183.2 11.1 %collective-permute-start.3 = (bf16[32,4096]{1,0:T(8,128)(2,1)}, bf16[32,4096]{1,0:T(8,128)(2,1)S(1)}, u32[]{:S(2)}, u32[]{:S(2)}) collective-permute-start(bf16[32,4096]{1,0:T(8,128)(2,1)} %get-tuple-element.10.refs_0_), channel_id=1, source_target_pairs={{0,1},{1,0},{2,3},{3,2},{4,5},{5,4},{6,7},{7,6},{8,9},{9,8},{10,11... | collective-permute-start | bytes 786440 | tf_op jit(solution)/shard_map/ppermute | solution.py:361
  (12 other events, 352.4 us)
Sparse Core Ops, SparseCore 0:
  10.9 134.0 all-gather.4
  211.8 67.4 all-gather.2
